TPU v7x, 32 devices: a whole 2x2x4 slice. The times are simulated.
32 devices in a mesh: ctx: 8 (over z, y), head: 4 (over x, core).
Axes of the slice: x: 2, y: 2, z: 4, core: 2. Of those that a mesh axis runs over, the one named last changes fastest.
Arguments:
- layer_input: bfloat16 [2048, 16384], P('ctx'), may hold values from -6 to 6
- queries: bfloat16 [2048, 8192], P('ctx', 'head'), may hold values from -80 to 80
- saved_keys: bfloat16 [2048, 512], P('ctx', 'head'), may hold values from -6 to 6
- saved_values: bfloat16 [2048, 512], P('ctx', 'head'), may hold values from -6 to 6
- grad_output: bfloat16 [2048, 8192], P('ctx', 'head'), may hold values from -6 to 6
- key_weight: bfloat16 [16384, 512], P(None, 'head'), may hold values from -0.25 to 0.25
- value_weight: bfloat16 [16384, 512], P(None, 'head'), may hold values from -0.25 to 0.25
- block_table: int32 [8, 2], replicated, may hold values from 0 to 15, as said below
Outputs:
- grad_queries: bfloat16 [2048, 8192], P('ctx', 'head')
- grad_key_weight: float32 [16384, 512], P('ctx', 'head')
- grad_value_weight: float32 [16384, 512], P('ctx', 'head')
- grad_input: bfloat16 [2048, 16384], P('ctx', 'head')
Inputs may be any that keep to these rules, and one draw needn't show every extreme that they name: `block_table`: row r holds a block b and its mirror 2 * 8 - 1 - b, in either order; every block of 0 to 15 appears exactly once.
All inputs are finite; a program needn't handle non-finite values.
Results may differ from a plain program's by a relative error of at most 0.02.
Values may be sent and summed in bfloat16 or wider, within the bound.
A program may use at most 128 MiB of HBM per device.

v0:
```python
import jax
import jax.numpy as jnp
from jax import lax
from jax.sharding import PartitionSpec as P

HD = 128
GRP = 16


def add_tile(accumulator, tile_grad, first_row):
    current = lax.dynamic_slice_in_dim(accumulator, first_row, tile_grad.shape[0], 0)
    return lax.dynamic_update_slice_in_dim(accumulator, current + tile_grad, first_row, 0)


def project_rows(columns, key_value):
    return lax.dot_general(
        columns, key_value, (((0,), (0,)), ((), ())), preferred_element_type=jnp.float32
    )


def local(
    layer_input,
    queries,
    saved_keys,
    saved_values,
    grad_output,
    key_weight,
    value_weight,
    block_table,
):
    devices = lax.axis_size("ctx")
    own_index = lax.axis_index("ctx")
    block_rows = queries.shape[0] // 2
    seq_total = 2 * block_rows * devices
    key_tile = min(512, seq_total)
    score_scale = HD ** (-0.5)
    all_keys, all_values = (
        lax.all_gather(saved_keys, "ctx", axis=0, tiled=True),
        lax.all_gather(saved_values, "ctx", axis=0, tiled=True),
    )
    block_list = block_table.reshape(-1)
    sorted_slots = jnp.argsort(block_list)
    keys_sorted = all_keys.reshape(2 * devices, block_rows, HD)[sorted_slots].reshape(seq_total, HD)
    values_sorted = all_values.reshape(2 * devices, block_rows, HD)[sorted_slots].reshape(
        seq_total, HD
    )
    tile_offsets = jnp.arange(key_tile, dtype=jnp.int32)
    grad_keys = jnp.zeros((seq_total, HD), jnp.float32)
    grad_values = jnp.zeros((seq_total, HD), jnp.float32)
    query_grads = []
    for slot_index in range(2):
        block_id = block_table[own_index, slot_index]
        local_queries = queries[slot_index * block_rows : (slot_index + 1) * block_rows].reshape(
            block_rows, GRP, HD
        )
        local_grads = grad_output[slot_index * block_rows : (slot_index + 1) * block_rows].reshape(
            block_rows, GRP, HD
        )
        query_pos = block_id * block_rows + jnp.arange(block_rows, dtype=jnp.int32)
        tile_count = ((block_id + 1) * block_rows + key_tile - 1) // key_tile

        def tile_logits(tile_index):
            first_row = tile_index * key_tile
            key_block = lax.dynamic_slice_in_dim(keys_sorted, first_row, key_tile, 0)
            logits = (
                jnp.einsum(
                    "thd,kd->htk", local_queries, key_block, preferred_element_type=jnp.float32
                )
                * score_scale
            )
            visible = (first_row + tile_offsets)[None, :] <= query_pos[:, None]
            return (jnp.where(visible[None], logits, -jnp.inf), first_row, key_block)

        def running_stats(tile_index, state):
            running_max, normalizer = state
            logits = tile_logits(tile_index)[0]
            updated = jnp.maximum(running_max, jnp.max(logits, axis=-1))
            normalizer = normalizer * jnp.exp(running_max - updated) + jnp.sum(
                jnp.exp(logits - updated[..., None]), axis=-1
            )
            return (updated, normalizer)

        start_max = jnp.full((GRP, block_rows), -jnp.inf, jnp.float32)
        start_norm = jnp.zeros((GRP, block_rows), jnp.float32)
        running_max, normalizer = lax.fori_loop(
            0, tile_count, running_stats, (start_max, start_norm)
        )
        log_norm = running_max + jnp.log(normalizer)

        def value_pass(tile_index, state):
            row_delta, value_acc = state
            logits, first_row, key_block = tile_logits(tile_index)
            value_block = lax.dynamic_slice_in_dim(values_sorted, first_row, key_tile, 0)
            probability = jnp.exp(logits - log_norm[..., None])
            grad_probs = jnp.einsum(
                "thd,kd->htk", local_grads, value_block, preferred_element_type=jnp.float32
            )
            row_delta = row_delta + jnp.sum(probability * grad_probs, axis=-1)
            tile_grad = jnp.einsum(
                "htk,thd->kd",
                probability.astype(jnp.bfloat16),
                local_grads,
                preferred_element_type=jnp.float32,
            )
            return (row_delta, add_tile(value_acc, tile_grad, first_row))

        row_delta, grad_values = lax.fori_loop(
            0, tile_count, value_pass, (jnp.zeros((GRP, block_rows), jnp.float32), grad_values)
        )

        def query_pass(tile_index, state):
            grad_query, key_acc = state
            logits, first_row, key_block = tile_logits(tile_index)
            value_block = lax.dynamic_slice_in_dim(values_sorted, first_row, key_tile, 0)
            probability = jnp.exp(logits - log_norm[..., None])
            grad_probs = jnp.einsum(
                "thd,kd->htk", local_grads, value_block, preferred_element_type=jnp.float32
            )
            grad_logits = (probability * (grad_probs - row_delta[..., None])).astype(jnp.bfloat16)
            grad_query = grad_query + jnp.einsum(
                "htk,kd->thd", grad_logits, key_block, preferred_element_type=jnp.float32
            )
            tile_grad = jnp.einsum(
                "htk,thd->kd", grad_logits, local_queries, preferred_element_type=jnp.float32
            )
            return (grad_query, add_tile(key_acc, tile_grad, first_row))

        start_query = jnp.zeros((block_rows, GRP, HD), jnp.float32)
        grad_query, grad_keys = lax.fori_loop(0, tile_count, query_pass, (start_query, grad_keys))
        query_grads.append(
            (grad_query * score_scale).astype(jnp.bfloat16).reshape(block_rows, GRP * HD)
        )
    grad_queries = jnp.concatenate(query_grads, axis=0)
    keys_device = (
        (grad_keys * score_scale)
        .reshape(2 * devices, block_rows, HD)[block_list]
        .reshape(seq_total, HD)
    )
    values_device = grad_values.reshape(2 * devices, block_rows, HD)[block_list].reshape(
        seq_total, HD
    )
    key_sums, value_sums = (
        lax.psum_scatter(
            keys_device.astype(jnp.bfloat16), "ctx", scatter_dimension=0, tiled=True
        ).astype(jnp.float32),
        lax.psum_scatter(
            values_device.astype(jnp.bfloat16), "ctx", scatter_dimension=0, tiled=True
        ).astype(jnp.float32),
    )
    grad_key_rows = key_sums.astype(jnp.bfloat16)
    grad_value_rows = value_sums.astype(jnp.bfloat16)
    key_value = jnp.concatenate([grad_key_rows, grad_value_rows], axis=1)
    gradients = lax.psum_scatter(
        project_rows(layer_input, key_value).astype(jnp.bfloat16),
        "ctx",
        scatter_dimension=0,
        tiled=True,
    ).astype(jnp.float32)
    grad_key_weight = gradients[:, :HD]
    grad_value_weight = gradients[:, HD:]
    contract = (((1,), (1,)), ((), ()))
    input_terms = lax.dot_general(
        grad_key_rows, key_weight, contract, preferred_element_type=jnp.float32
    )
    input_terms = input_terms + lax.dot_general(
        grad_value_rows, value_weight, contract, preferred_element_type=jnp.float32
    )
    grad_input = lax.psum_scatter(
        input_terms.astype(jnp.bfloat16), "head", scatter_dimension=1, tiled=True
    )
    return (grad_queries, grad_key_weight, grad_value_weight, grad_input)


def solution(mesh):
    in_specs = (
        P("ctx", None),
        P("ctx", "head"),
        P("ctx", "head"),
        P("ctx", "head"),
        P("ctx", "head"),
        P(None, "head"),
        P(None, "head"),
        P(),
    )
    out_specs = (P("ctx", "head"), P("ctx", "head"), P("ctx", "head"), P("ctx", "head"))
    return jax.shard_map(local, mesh=mesh, in_specs=in_specs, out_specs=out_specs, check_vma=False)
```

profile of v0, /device:TPU:29, one launch (start us, length us, event | category | flops | bytes accessed | tf_op | source)
XLA Modules:
  0.0 519.6 jit_solution(11411842517695448279)
XLA Ops:
  13.4 25.6 %all_gather.6 = bf16[2048,128]{1,0:T(8,128)(2,1)S(1)} all-gather(bf16[256,128]{1,0:T(8,128)(2,1)} %param.22), channel_id=1, replica_groups=mesh['ctx'=8,'head'=4] {'ctx'}, dimensions={0}, use_global_device_ids=true | all-gather | bytes 589824 | tf_op jit(solution)/shard_map/all_gather | solution.py:38
  38.9 2.1 fusion.127
  42.3 5.4 %while.78 = (s32[]{:T(128)}, f32[16,128]{1,0:T(8,128)S(1)}, f32[16,128]{1,0:T(8,128)S(1)}, s32[]{:T(128)}, bf16[2048,128]{1,0:T(8,128)(2,1)S(1)}, /*index=5*/bf1...) while((s32[]{:T(128)}, f32[16,128]{1,0:T(8,128)S(1)}, ...), condition=%wide.region_4.5_spmd.clone, body=%wide.region_1.4_spmd.clone.sunk | while | flops 275845760 | bytes 9352359 | solution.py:85
  47.7 25.0 %all_gather.7 = bf16[2048,128]{1,0:T(8,128)(2,1)S(1)} all-gather(bf16[256,128]{1,0:T(8,128)(2,1)S(1)} %copy-done.11), channel_id=1, replica_groups=mesh['ctx'=8,'head'=4] {'ctx'}, dimensions={0}, use_global_device_ids=true | all-gather | bytes 589824 | tf_op jit(solution)/shard_map/all_gather | solution.py:39
  75.7 12.3 %while.79 = (s32[]{:T(128)}, f32[16,128]{1,0:T(8,128)S(1)}, f32[2048,128]{1,0:T(8,128)S(1)}, s32[]{:T(128)}, bf16[2048,128]{1,0:T(8,128)(2,1)S(1)}, /*index=5*/b...) while((s32[]{:T(128)}, f32[16,128]{1,0:T(8,128)S(1)}, ...), condition=%wide.region_7.8_spmd.clone, body=%wide.region_5.7_spmd.clone.sunk | while | flops 814875264 | bytes 15193287 | solution.py:107
  77.6 2.1 fusion.207
  81.7 2.1 fusion.207
  85.8 2.1 fusion.207
  89.4 3.6 while.81
  95.4 8.7 %while.82 = (s32[]{:T(128)}, f32[16,128]{1,0:T(8,128)S(1)}, f32[2048,128]{1,0:T(8,128)S(1)}, s32[]{:T(128)}, bf16[2048,128]{1,0:T(8,128)(2,1)S(1)}, /*index=5*/b...) while((s32[]{:T(128)}, f32[16,128]{1,0:T(8,128)S(1)}, ...), condition=%wide.region_16.17_spmd.clone, body=%wide.region_14.16_spmd.clone.sunk | while | flops 814875264 | bytes 17290468 | solution.py:107
  97.7 2.1 fusion.230
  101.9 2.1 fusion.230
  106.2 18.3 %while.80 = (s32[]{:T(128)}, f32[128,16,128]{0,2,1:T(8,128)S(1)}, f32[2048,128]{1,0:T(8,128)}, s32[]{:T(128)}, bf16[2048,128]{1,0:T(8,128)(2,1)S(1)}, /*index=5*...) while((s32[]{:T(128)}, f32[128,16,128]{0,2,1:T(8,128)S(1)}, ...), condition=%wide.region_9.10_spmd.clone, body=%wide.region_8.9_spmd.clone.sunk | while | flops 1080427136 | bytes 19420372 | solution.py:129
  107.1 2.3 fusion.218
  109.4 2.4 fusion.220
  113.2 2.3 fusion.218
  115.5 2.4 fusion.220
  119.3 2.3 fusion.218
  121.6 2.4 fusion.220
  125.6 12.5 %while.83 = (s32[]{:T(128)}, f32[128,16,128]{0,2,1:T(8,128)S(1)}, f32[2048,128]{1,0:T(8,128)}, s32[]{:T(128)}, bf16[2048,128]{1,0:T(8,128)(2,1)S(1)}, /*index=5*...) while((s32[]{:T(128)}, f32[128,16,128]{0,2,1:T(8,128)S(1)}, ...), condition=%wide.region_18.19_spmd.clone, body=%wide.region_17.18_spmd.clone.sunk | while | flops 1080427136 | bytes 21517552 | solution.py:129
  126.6 2.3 fusion.241
  128.9 2.4 fusion.243
  132.9 2.3 fusion.241
  135.2 2.4 fusion.243
  140.9 2.6 gather_fusion.3
  143.8 68.9 %reduce-scatter.5.cloned.1.call-done = bf16[256,128]{1,0:T(8,128)(2,1)} async-done(((bf16[2048,128]{1,0:T(8,128)(2,1)}), bf16[256,128]{1,0:T(8,128)(2,1)}) %reduce-scatter.5.cloned.1.call-update) | async-done | bytes 65552 | tf_op jit(solution)/shard_map/reduce_scatter | solution.py:143
  212.7 65.2 %reduce-scatter.7.cloned.1.call-done = bf16[256,128]{1,0:T(8,128)(2,1)} async-done(((bf16[2048,128]{1,0:T(8,128)(2,1)}), bf16[256,128]{1,0:T(8,128)(2,1)}) %reduce-scatter.7.cloned.1.call-update) | async-done | bytes 65552 | tf_op jit(solution)/shard_map/reduce_scatter | solution.py:146
  278.0 9.1 %fusion.119 = bf16[16384,256]{0,1:T(8,128)(2,1)} fusion(bf16[256,16384]{1,0:T(8,128)(2,1)} %param.20, bf16[256,128]{1,0:T(8,128)(2,1)} %reduce-scatter.7.cloned.1.call-done, bf16[256,128]{1,0:T(8,128)(2,1)} %reduce-scatter.5.cloned.1.call-done), kind=kOutput, calls=%fused_computation.135 | convolution fusion | flops 2151940096 | bytes 16908288 | tf_op jit(solution)/shard_map/dot_general | solution.py:16
  287.9 10.8 %fusion.128 = f32[256,16384]{1,0:T(8,128)} fusion(bf16[256,128]{1,0:T(8,128)(2,1)S(1)} %copy-done.9, bf16[16384,128]{1,0:T(8,128)(2,1)} %param.25), kind=kOutput, calls=%fused_computation.156 | convolution fusion | flops 1073741824 | bytes 21037056 | tf_op jit(solution)/shard_map/dot_general | solution.py:162
  298.7 12.7 %fusion.118 = bf16[256,16384]{1,0:T(8,128)(2,1)} fusion(f32[256,16384]{1,0:T(8,128)} %fusion.128, bf16[256,128]{1,0:T(8,128)(2,1)S(1)} %copy-done.10, bf16[16384,128]{1,0:T(8,128)(2,1)} %param.26), kind=kOutput, calls=%fused_computation.133 | convolution fusion | flops 1082130432 | bytes 29425664 | tf_op jit(solution)/shard_map/dot_general | solution.py:165
  314.0 123.5 %reduce-scatter.9.cloned.1.call-done = bf16[2048,256]{0,1:T(8,128)(2,1)} async-done(((bf16[16384,256]{0,1:T(8,128)(2,1)}), bf16[2048,256]{0,1:T(8,128)(2,1)}) %reduce-scatter.9.cloned.1.call-update) | async-done | bytes 1048592 | tf_op jit(solution)/shard_map/reduce_scatter | solution.py:153
  441.6 71.5 %reduce-scatter.11.cloned.1.call-done = bf16[256,4096]{1,0:T(8,128)(2,1)} async-done(((bf16[256,16384]{1,0:T(8,128)(2,1)}), bf16[256,4096]{1,0:T(8,128)(2,1)}) %reduce-scatter.11.cloned.1.call-update) | async-done | bytes 2097168 | tf_op jit(solution)/shard_map/reduce_scatter | solution.py:168
  (174 shorter events, 50.4 us)
Async XLA Ops:
  7.2 205.6 %reduce-scatter.5.cloned.1.call-start = ((), (), s32[]{:S(2)}) async-start(), calls=%async_computation.4 | async-start | bytes 589824 | tf_op jit(solution)/shard_map/reduce_scatter | solution.py:143
  42.3 5.5 %copy-start.11 = (bf16[256,128]{1,0:T(8,128)(2,1)S(1)}, bf16[256,128]{1,0:T(8,128)(2,1)}, u32[]{:S(2)}) copy-start(bf16[256,128]{1,0:T(8,128)(2,1)} %param.23) | copy-start | bytes 196612
  42.3 31.9 %copy-start.4 = (bf16[256,2048]{1,0:T(8,128)(2,1)S(1)}, bf16[256,2048]{1,0:T(8,128)(2,1)}, u32[]{:S(2)}) copy-start(bf16[256,2048]{1,0:T(8,128)(2,1)} %param.24) | copy-start | bytes 3145732
  75.7 13.1 %copy-start.3 = (bf16[128,2048]{1,0:T(8,128)(2,1)S(1)}, bf16[128,2048]{1,0:T(8,128)(2,1)}, u32[]{:S(2)}) copy-start(bf16[128,2048]{1,0:T(8,128)(2,1)} %get-tuple-element.678) | copy-start | bytes 1572868
  88.0 0.8 copy-start.5
  95.4 10.8 %copy-start.6 = (bf16[128,16,128]{2,0,1:T(8,128)(2,1)S(1)}, bf16[128,16,128]{2,0,1:T(8,128)(2,1)}, u32[]{:S(2)}) copy-start(bf16[128,16,128]{2,0,1:T(8,128)(2,1)} %copy-done.5) | copy-start | bytes 1572868
  95.6 1.0 copy-start.7
  99.9 1.0 copy-start.7
  104.1 1.0 copy-start.2
  124.5 1.0 copy-start
  125.6 1.0 copy-start.8
  131.8 1.0 copy-start.8
  140.8 137.1 %reduce-scatter.7.cloned.1.call-start = ((), (), s32[]{:S(2)}) async-start(), calls=%async_computation.5 | async-start | bytes 589824 | tf_op jit(solution)/shard_map/reduce_scatter | solution.py:146
  143.5 294.0 %reduce-scatter.9.cloned.1.call-start = ((), (), s32[]{:S(2)}) async-start(), calls=%async_computation.6 | async-start | bytes 9437184 | tf_op jit(solution)/shard_map/reduce_scatter | solution.py:153
  287.0 0.8 copy-start.9
  287.1 11.6 %copy-start.10 = (bf16[256,128]{1,0:T(8,128)(2,1)S(1)}, bf16[256,128]{1,0:T(8,128)(2,1)}, u32[]{:S(2)}) copy-start(bf16[256,128]{1,0:T(8,128)(2,1)} %reduce-scatter.7.cloned.1.call-done) | copy-start | bytes 196612
  287.1 226.0 %reduce-scatter.11.cloned.1.call-start = ((), (), s32[]{:S(2)}) async-start(), calls=%async_computation.7 | async-start | bytes 10485760 | tf_op jit(solution)/shard_map/reduce_scatter | solution.py:168
  311.4 1.2 copy-start.1
Sparse Core Ops, SparseCore 0:
  141.0 71.7 reduce-scatter.4
  217.0 60.9 reduce-scatter.6
  287.2 150.3 reduce-scatter.8
  440.7 72.3 reduce-scatter.10
where the time goes:
time: 523 us; the launch traced here: 520 us
  waiting for transfers between devices  329 us (63%)
  matrix products  84.9 us (16%)
  blocking collectives  50.5 us (10%)
  local copies, waits for them, and re-layouts  26 us (5%)
  between operations  16.7 us (3%)
  other arithmetic  10.4 us (2%)
    reduce_scatter x1, waiting for transfers between devices, local(): lax.psum_scatter(project_rows(layer_input, key_value).astype(jnp.bfloat16...  124 us
    reduce_scatter x1, waiting for transfers between devices, local(): lax.psum_scatter(input_terms.astype(jnp.bfloat16), 'head', scatter_dimens...  71.5 us
    reduce_scatter x1, waiting for transfers between devices, local(): lax.psum_scatter(keys_device.astype(jnp.bfloat16), 'ctx', scatter_dimensi...  68.9 us
    reduce_scatter x1, waiting for transfers between devices, local(): lax.psum_scatter(values_device.astype(jnp.bfloat16), 'ctx', scatter_dimen...  65.2 us
    all_gather x1, blocking collectives, local(): lax.all_gather(saved_keys, 'ctx', axis=0, tiled=True)  25.6 us
    all_gather x1, blocking collectives, local(): lax.all_gather(saved_values, 'ctx', axis=0, tiled=True)  25 us
    dot_general x1, matrix products, local(): lax.dot_general(grad_value_rows, value_weight, contract, preferred_elemen...  12.7 us
    dot_general x5, matrix products, query_pass(): jnp.einsum('htk,thd->kd', grad_logits, local_queries, preferred_element_t...  12 us
  transfers between devices with their start and end apart: 4, of which 4 were waited for; matrix products, arithmetic and copies ran while one was open for 6% of the time, Pallas kernels for 0%

commit v1 on v0

v1 whole, which is shorter than its diff:
```python
import functools
import math

import jax
import jax.numpy as jnp
from jax import lax
from jax.experimental import pallas as pl
from jax.experimental.pallas import tpu as pltpu
from jax.sharding import PartitionSpec as P

HD = 128
MESH = pl.DeviceIdType.MESH
NT = (((1,), (1,)), ((), ()))
NN = (((1,), (0,)), ((), ()))


def kernel(
    n_ctx,
    n_head,
    table,
    inverse,
    q_ref,
    g_ref,
    kv_ref,
    x_ref,
    kw_ref,
    vw_ref,
    dq_ref,
    x_all,
    w_all,
    rows_all,
    rows_heads,
    kv_all,
    keys,
    values,
    keys_t,
    scores,
    dprobs,
    acc_k,
    acc_v,
    part,
    received,
    own_rows,
    gather_send,
    gather_recv,
    x_send,
    x_recv,
    pair_send,
    pair_recv,
    w_send,
    w_recv,
    sum_send,
    sum_recv,
    rows_send,
    rows_recv,
    heads_send,
    heads_recv,
    local_sem,
):
    me = lax.axis_index("ctx")
    head = lax.axis_index("head")
    core = lax.rem(head, 2)
    partner = head + 1 - 2 * core
    tokens = q_ref.shape[0]
    blk = tokens // 2
    heads = q_ref.shape[1] // HD
    seq = tokens * n_ctx
    blocks = 2 * n_ctx
    cols = x_ref.shape[1] // n_ctx
    half = cols // 2
    feats = kw_ref.shape[0] // n_head
    scale = HD**-0.5
    log2_scale = scale * math.log2(math.e)

    def ctx_peer(d):
        return lax.rem(me + d, n_ctx)

    def ctx_source(d):
        return lax.rem(me + n_ctx - d, n_ctx)

    def head_peer(d):
        return lax.rem(head + d, n_head)

    def ctx_copy(src, dst, send, recv, d):
        return pltpu.make_async_remote_copy(
            src_ref=src,
            dst_ref=dst,
            send_sem=send.at[d],
            recv_sem=recv.at[d],
            device_id=(ctx_peer(d), head),
            device_id_type=MESH,
        )

    def head_copy(src, dst, send, recv, at, to):
        return pltpu.make_async_remote_copy(
            src_ref=src,
            dst_ref=dst,
            send_sem=send.at[at],
            recv_sem=recv.at[at],
            device_id=(me, to),
            device_id_type=MESH,
        )

    barrier = pltpu.get_barrier_semaphore()
    for d in range(1, n_ctx):
        pl.semaphore_signal(barrier, inc=1, device_id=(ctx_peer(d), head), device_id_type=MESH)
    for d in range(1, n_head):
        pl.semaphore_signal(barrier, inc=1, device_id=(me, head_peer(d)), device_id_type=MESH)
    pl.semaphore_wait(barrier, n_ctx + n_head - 2)

    own = pl.ds(pl.multiple_of(me * tokens, tokens), tokens)
    gathers = [
        ctx_copy(kv_ref, kv_all.at[pl.ds(2 * me, 2)], gather_send, gather_recv, d) for d in range(1, n_ctx)
    ]
    for copy in gathers:
        copy.start()
    locals_ = [
        pltpu.make_async_copy(
            x_ref.at[:, pl.ds(pl.multiple_of(me * cols, cols), cols)],
            x_all.at[own],
            local_sem.at[0],
        )
    ]
    own_feats = pl.ds(pl.multiple_of(head * feats, feats), feats)
    for i, ref in enumerate((kw_ref, vw_ref)):
        locals_.append(
            pltpu.make_async_copy(
                ref.at[own_feats],
                w_all.at[:, pl.ds(pl.multiple_of((head * 2 + i) * HD, HD), HD)],
                local_sem.at[1 + i],
            )
        )
    for copy in locals_:
        copy.start()
    kv_all[pl.ds(2 * me, 2)] = kv_ref[...]
    for copy in gathers:
        copy.wait()

    x_copies = []
    for d in range(1, n_ctx):
        first = ctx_peer(d) * cols + core * half
        x_copies.append(
            ctx_copy(
                x_ref.at[:, pl.ds(pl.multiple_of(first, half), half)],
                x_all.at[own, pl.ds(pl.multiple_of(core * half, half), half)],
                x_send,
                x_recv,
                d,
            )
        )
    w_copies = []
    for d in range(1, n_head):
        to = head_peer(d)
        for i, ref in enumerate((kw_ref, vw_ref)):
            w_copies.append(
                head_copy(
                    ref.at[pl.ds(pl.multiple_of(to * feats, feats), feats)],
                    w_all.at[:, pl.ds(pl.multiple_of((head * 2 + i) * HD, HD), HD)],
                    w_send,
                    w_recv,
                    2 * d + i,
                    to,
                )
            )
    for copy in x_copies + w_copies:
        copy.start()

    def sort_block(u, carry):
        from_rows = kv_all[inverse[u]]
        to_rows = pl.ds(pl.multiple_of(u * blk, blk), blk)
        keys[to_rows, :] = from_rows[:, :HD]
        values[to_rows, :] = from_rows[:, HD:]
        keys_t[:, to_rows] = from_rows[:, :HD].T
        return carry

    lax.fori_loop(0, blocks, sort_block, 0)
    acc_k[...] = jnp.zeros_like(acc_k)
    acc_v[...] = jnp.zeros_like(acc_v)

    block_0 = table[2 * me]
    block_1 = table[2 * me + 1]
    top_block = jnp.maximum(block_0, block_1)
    chunk = min(512, seq // 2)
    width = 2 * blk

    first_is_top = jnp.full((width, HD), block_0, jnp.int32) == top_block

    def load(ref, pair):
        halves = []
        for slot in range(2):
            rows = slice(slot * blk, (slot + 1) * blk)
            halves.append(
                jnp.concatenate(
                    [
                        ref[rows, pl.ds(pl.multiple_of((2 * pair + i) * HD, HD), HD)]
                        for i in range(2)
                    ],
                    axis=0,
                ).astype(jnp.float32)
            )
        first, second = halves
        return (
            jnp.where(first_is_top, first, second).astype(jnp.bfloat16),
            jnp.where(first_is_top, second, first).astype(jnp.bfloat16),
        )

    def attend(q, g, block_id, extent, free):
        top = None
        for start in range(0, extent, chunk):
            rows = slice(start, start + chunk)
            s = lax.dot_general(keys[rows, :], q, NT, preferred_element_type=jnp.float32)
            if start + chunk > free:
                key_pos = lax.broadcasted_iota(jnp.int32, (chunk, width), 0)
                row_pos = lax.rem(lax.broadcasted_iota(jnp.int32, (chunk, width), 1), blk)
                s = jnp.where(key_pos - row_pos <= block_id * blk - start, s, -1e30)
            scores[rows, :] = s
            here = jnp.max(s, axis=0, keepdims=True)
            top = here if top is None else jnp.maximum(top, here)
        top = top * log2_scale
        norm = jnp.zeros((1, width), jnp.float32)
        delta = jnp.zeros((1, width), jnp.float32)
        for start in range(0, extent, chunk):
            rows = slice(start, start + chunk)
            prob = jnp.exp2(scores[rows, :] * log2_scale - top)
            dp = lax.dot_general(values[rows, :], g, NT, preferred_element_type=jnp.float32)
            norm = norm + jnp.sum(prob, axis=0, keepdims=True)
            delta = delta + jnp.sum(prob * dp, axis=0, keepdims=True)
            scores[rows, :] = prob
            dprobs[rows, :] = dp
        inv = 1.0 / norm
        delta = delta * inv
        dq_t = jnp.zeros((HD, width), jnp.float32)
        for start in range(0, extent, chunk):
            rows = slice(start, start + chunk)
            prob = scores[rows, :] * inv
            ds = (prob * (dprobs[rows, :] - delta)).astype(jnp.bfloat16)
            pieces = slice(start // blk, (start + chunk) // blk)
            acc_v[pieces] += lax.dot_general(
                prob.astype(jnp.bfloat16), g, NN, preferred_element_type=jnp.float32
            ).reshape(-1, blk, HD)
            acc_k[pieces] += lax.dot_general(
                ds, q, NN, preferred_element_type=jnp.float32
            ).reshape(-1, blk, HD)
            dq_t = dq_t + lax.dot_general(
                keys_t[:, rows], ds, NN, preferred_element_type=jnp.float32
            )
        return jnp.concatenate(
            [dq_t[:, i * blk : (i + 1) * blk].T for i in range(2)], axis=0
        ) * scale

    def head_pair(pair, carry):
        q_top, q_low = load(q_ref, pair)
        g_top, g_low = load(g_ref, pair)
        top_grad = attend(q_top, g_top, top_block, seq, seq // 2)
        low_grad = attend(q_low, g_low, blocks - 1 - top_block, seq // 2, 0)
        for slot, grads in enumerate(
            (
                jnp.where(first_is_top, top_grad, low_grad),
                jnp.where(first_is_top, low_grad, top_grad),
            )
        ):
            for i in range(2):
                dq_ref[
                    slot * blk : (slot + 1) * blk,
                    pl.ds(pl.multiple_of((2 * pair + i) * HD, HD), HD),
                ] = grads[i * blk : (i + 1) * blk].astype(jnp.bfloat16)
        return carry

    lax.fori_loop(0, heads // 2, head_pair, 0)

    def unsort(s, carry):
        to_rows = pl.ds(pl.multiple_of(s * blk, blk), blk)
        part[to_rows, :HD] = (acc_k[table[s]] * scale).astype(jnp.bfloat16)
        part[to_rows, HD:] = acc_v[table[s]].astype(jnp.bfloat16)
        return carry

    lax.fori_loop(0, blocks, unsort, 0)

    sums = []
    for d in range(1, n_ctx):
        to_rows = pl.ds(pl.multiple_of(ctx_peer(d) * tokens, tokens), tokens)
        sums.append(ctx_copy(part.at[to_rows], received.at[d], sum_send, sum_recv, d))
    for copy in sums:
        copy.start()
    for copy in sums:
        copy.wait()
    total = part[own, :].astype(jnp.float32)
    for d in range(1, n_ctx):
        total = total + received[d].astype(jnp.float32)
    own_rows[...] = total.astype(jnp.bfloat16)

    head_cols = pl.ds(pl.multiple_of(head * 2 * HD, 2 * HD), 2 * HD)
    locals_.append(pltpu.make_async_copy(own_rows, rows_all.at[own], local_sem.at[3]))
    locals_.append(pltpu.make_async_copy(own_rows, rows_heads.at[:, head_cols], local_sem.at[4]))
    for copy in locals_[3:]:
        copy.start()
    rows_copies = [
        ctx_copy(own_rows, rows_all.at[own], rows_send, rows_recv, d) for d in range(1, n_ctx)
    ]
    for d in range(1, n_head):
        rows_copies.append(
            head_copy(
                own_rows, rows_heads.at[:, head_cols], heads_send, heads_recv, d, head_peer(d)
            )
        )
    for copy in rows_copies:
        copy.start()

    pair_copies = []
    for d in range(1, n_ctx):
        x_copies[d - 1].wait()
        source = ctx_source(d)
        piece = x_all.at[
            pl.ds(pl.multiple_of(source * tokens, tokens), tokens),
            pl.ds(pl.multiple_of(core * half, half), half),
        ]
        copy = head_copy(piece, piece, pair_send, pair_recv, d, partner)
        copy.start()
        pair_copies.append(copy)
    for copy in w_copies + rows_copies + pair_copies + locals_:
        copy.wait()


def local(
    n_ctx,
    n_head,
    layer_input,
    queries,
    saved_keys,
    saved_values,
    grad_output,
    key_weight,
    value_weight,
    block_table,
):
    tokens = queries.shape[0]
    blk = tokens // 2
    seq = tokens * n_ctx
    cols = layer_input.shape[1] // n_ctx
    feats = key_weight.shape[0] // n_head
    table = block_table.reshape(-1)
    slots = jnp.arange(table.shape[0], dtype=jnp.int32)
    inverse = jnp.sum(jnp.where(table[None, :] == slots[:, None], slots[None, :], 0), axis=1)
    saved = jnp.concatenate([saved_keys, saved_values], axis=1).reshape(2, blk, 2 * HD)
    smem = pl.BlockSpec(memory_space=pltpu.SMEM)
    vmem = pl.BlockSpec(memory_space=pltpu.VMEM)
    hbm = pl.BlockSpec(memory_space=pl.ANY)
    bf16 = jnp.bfloat16
    f32 = jnp.float32
    dma = pltpu.SemaphoreType.DMA
    dq, x_all, w_all, rows_all, rows_heads = pl.pallas_call(
        functools.partial(kernel, n_ctx, n_head),
        out_shape=(
            jax.ShapeDtypeStruct(queries.shape, bf16),
            jax.ShapeDtypeStruct((seq, cols), bf16),
            jax.ShapeDtypeStruct((feats, n_head * 2 * HD), bf16),
            jax.ShapeDtypeStruct((seq, 2 * HD), bf16),
            jax.ShapeDtypeStruct((tokens, n_head * 2 * HD), bf16),
        ),
        in_specs=[smem, smem, vmem, vmem, vmem, hbm, hbm, hbm],
        out_specs=(vmem, hbm, hbm, hbm, hbm),
        scratch_shapes=[
            pltpu.VMEM((2 * n_ctx, blk, 2 * HD), bf16),
            pltpu.VMEM((seq, HD), bf16),
            pltpu.VMEM((seq, HD), bf16),
            pltpu.VMEM((HD, seq), bf16),
            pltpu.VMEM((seq, 2 * blk), f32),
            pltpu.VMEM((seq, 2 * blk), f32),
            pltpu.VMEM((2 * n_ctx, blk, HD), f32),
            pltpu.VMEM((2 * n_ctx, blk, HD), f32),
            pltpu.VMEM((seq, 2 * HD), bf16),
            pltpu.VMEM((n_ctx, tokens, 2 * HD), bf16),
            pltpu.VMEM((tokens, 2 * HD), bf16),
            dma((n_ctx,)),
            dma((n_ctx,)),
            dma((n_ctx,)),
            dma((n_ctx,)),
            dma((n_ctx,)),
            dma((n_ctx,)),
            dma((2 * n_head,)),
            dma((2 * n_head,)),
            dma((n_ctx,)),
            dma((n_ctx,)),
            dma((n_ctx,)),
            dma((n_ctx,)),
            dma((n_head,)),
            dma((n_head,)),
            dma((5,)),
        ],
        compiler_params=pltpu.CompilerParams(
            collective_id=0, has_side_effects=True, vmem_limit_bytes=48 * 1024 * 1024
        ),
    )(table, inverse, queries, grad_output, saved, layer_input, key_weight, value_weight)
    contract = (((0,), (0,)), ((), ()))
    gradients = lax.dot_general(x_all, rows_all, contract, preferred_element_type=f32)
    grad_input = lax.dot_general(rows_heads, w_all, NT, preferred_element_type=f32).astype(bf16)
    return dq, gradients[:, :HD], gradients[:, HD:], grad_input


def solution(mesh):
    both = P("ctx", "head")
    in_specs = (P("ctx", None), both, both, both, both, P(None, "head"), P(None, "head"), P())
    out_specs = (both, both, both, both)
    return jax.shard_map(
        functools.partial(local, mesh.shape["ctx"], mesh.shape["head"]),
        mesh=mesh,
        in_specs=in_specs,
        out_specs=out_specs,
        check_vma=False,
    )
```

time: 523 us -> 210 us (0.40)
  the two profiles are of different devices: /device:TPU:29 before, /device:TPU:14 now
where the time goes in v1:
time: 210 us
  Pallas kernels  192 us (91%)
  matrix products  9.83 us (5%)
  local copies, waits for them, and re-layouts  5.7 us (3%)
    pallas_call x1, Pallas kernels, local(): pl.pallas_call(functools.partial(kernel, n_ctx, n_head), out_shape=(jax.S...  192 us
    dot_general x1, matrix products, local(): lax.dot_general(x_all, rows_all, contract, preferred_element_type=f32)  6.14 us

profile of v1, /device:TPU:14, one launch (start us, length us, event | category | flops | bytes accessed | tf_op | source)
XLA Modules:
  0.0 209.7 jit_solution(5698638702373748809)
XLA Ops:
  0.6 0.8 copy.14
  1.4 0.1 reshape.15.table
  1.5 0.1 select_reduce_fusion.inverse
  1.6 0.9 pad_maximum_fusion
  2.5 0.0 copy-start
  2.5 1.2 copy-done
  3.7 0.0 copy-start.1
  3.7 1.2 copy-done.1
  4.9 192.5 %shard_map.111 = (bf16[256,2048]{1,0:T(8,128)(2,1)S(1)}, bf16[2048,2048]{1,0:T(8,128)(2,1)}, bf16[4096,1024]{1,0:T(8,128)(2,1)}, bf16[2048,256]{1,0:T(8,128)(2,1)S(1)}, bf16[256,1024]{1,0:T(8,128)(2,1)S(1)}) custom-call(s32[16]{0:T(128)S(1)} %reshape.15.table, s32[16]{0:T(128)S(1)} %select_reduce_fusion.inverse, bf16[256,2048]{1,0:T(8,128)(2,1)S(1)} %copy-done, ...), custom_call_target="tpu_custom_call" | custom-call | tf_op jit(solution)/shard_map/pallas_call | solution.py:351
  197.4 0.0 copy-start.2
  197.4 6.1 %fusion.1 = f32[2048,256]{1,0:T(8,128)S(1)} fusion(bf16[2048,2048]{1,0:T(8,128)(2,1)} %get-tuple-element.10, bf16[2048,256]{1,0:T(8,128)(2,1)S(1)} %get-tuple-element.11), kind=kOutput, calls=%fused_computation.5 | convolution fusion | flops 2147483648 | bytes 11534336 | tf_op jit(solution)/shard_map/dot_general | solution.py:395
  203.6 1.5 fusion
  205.0 0.0 copy-done.2
  205.0 3.7 %convolution_convert_fusion = bf16[256,4096]{1,0:T(8,128)(2,1)} fusion(bf16[256,1024]{1,0:T(8,128)(2,1)S(1)} %get-tuple-element.12, bf16[4096,1024]{1,0:T(8,128)(2,1)S(1)} %copy-done.2), kind=kOutput, calls=%fused_computation | convolution fusion | flops 2148532224 | bytes 11010048 | tf_op jit(solution)/shard_map/dot_general | solution.py:396
  208.7 1.0 copy.16
Async XLA Ops:
  2.5 1.2 copy-start
  3.7 1.2 copy-start.1
  197.4 7.6 %copy-start.2 = (bf16[4096,1024]{1,0:T(8,128)(2,1)S(1)}, bf16[4096,1024]{1,0:T(8,128)(2,1)}, u32[]{:S(2)}) copy-start(bf16[4096,1024]{1,0:T(8,128)(2,1)} %get-tuple-element.13) | copy-start | bytes 25165828

commit v2 on v1

--- a/solution.py
+++ b/solution.py
@@ -41,8 +41,16 @@
     part,
     received,
     own_rows,
+    paired,
+    outgoing,
     gather_send,
     gather_recv,
+    gather_pair_send,
+    gather_pair_recv,
+    side_send,
+    side_recv,
+    side_pair_send,
+    side_pair_recv,
     x_send,
     x_recv,
     pair_send,
@@ -51,8 +59,12 @@
     w_recv,
     sum_send,
     sum_recv,
+    sum_pair_send,
+    sum_pair_recv,
     rows_send,
     rows_recv,
+    rows_pair_send,
+    rows_pair_recv,
     heads_send,
     heads_recv,
     local_sem,
@@ -61,6 +73,10 @@
     head = lax.axis_index("head")
     core = lax.rem(head, 2)
     partner = head + 1 - 2 * core
+    side = lax.rem(head // 2, 2)
+    across = head + 2 - 4 * side
+    ctx_partner = me + 1 - 2 * lax.rem(me, 2)
+    strides = n_ctx // 2
     tokens = q_ref.shape[0]
     blk = tokens // 2
     heads = q_ref.shape[1] // HD
@@ -81,15 +97,35 @@
     def head_peer(d):
         return lax.rem(head + d, n_head)
 
-    def ctx_copy(src, dst, send, recv, d):
+    def ctx_copy(src, dst, send, recv, at, to):
         return pltpu.make_async_remote_copy(
             src_ref=src,
             dst_ref=dst,
-            send_sem=send.at[d],
-            recv_sem=recv.at[d],
-            device_id=(ctx_peer(d), head),
+            send_sem=send.at[at],
+            recv_sem=recv.at[at],
+            device_id=(to, head),
             device_id_type=MESH,
         )
+
+    def gather(src, place, sems):
+        direct = [
+            ctx_copy(src, place(me), sems[0], sems[1], k, ctx_peer(2 * k))
+            for k in range(1, strides)
+        ]
+        passed = [ctx_copy(src, place(me), sems[2], sems[3], 0, ctx_partner)]
+        for copy in direct + passed:
+            copy.start()
+        return direct, passed
+
+    def gather_on(direct, passed, place, sems):
+        for k in range(1, strides):
+            direct[k - 1].wait()
+            piece = place(ctx_source(2 * k))
+            copy = ctx_copy(piece, piece, sems[2], sems[3], k, ctx_partner)
+            copy.start()
+            passed.append(copy)
+        for copy in passed:
+            copy.wait()
 
     def head_copy(src, dst, send, recv, at, to):
         return pltpu.make_async_remote_copy(
@@ -109,45 +145,11 @@
     pl.semaphore_wait(barrier, n_ctx + n_head - 2)
 
     own = pl.ds(pl.multiple_of(me * tokens, tokens), tokens)
-    gathers = [
-        ctx_copy(kv_ref, kv_all.at[pl.ds(2 * me, 2)], gather_send, gather_recv, d) for d in range(1, n_ctx)
-    ]
-    for copy in gathers:
-        copy.start()
-    locals_ = [
-        pltpu.make_async_copy(
-            x_ref.at[:, pl.ds(pl.multiple_of(me * cols, cols), cols)],
-            x_all.at[own],
-            local_sem.at[0],
-        )
-    ]
-    own_feats = pl.ds(pl.multiple_of(head * feats, feats), feats)
-    for i, ref in enumerate((kw_ref, vw_ref)):
-        locals_.append(
-            pltpu.make_async_copy(
-                ref.at[own_feats],
-                w_all.at[:, pl.ds(pl.multiple_of((head * 2 + i) * HD, HD), HD)],
-                local_sem.at[1 + i],
-            )
-        )
-    for copy in locals_:
-        copy.start()
-    kv_all[pl.ds(2 * me, 2)] = kv_ref[...]
-    for copy in gathers:
-        copy.wait()
-
-    x_copies = []
-    for d in range(1, n_ctx):
-        first = ctx_peer(d) * cols + core * half
-        x_copies.append(
-            ctx_copy(
-                x_ref.at[:, pl.ds(pl.multiple_of(first, half), half)],
-                x_all.at[own, pl.ds(pl.multiple_of(core * half, half), half)],
-                x_send,
-                x_recv,
-                d,
-            )
-        )
+    def kv_place(source):
+        return kv_all.at[pl.ds(2 * source, 2)]
+
+    kv_sems = (gather_send, gather_recv, gather_pair_send, gather_pair_recv)
+    kv_direct, kv_passed = gather(kv_ref, kv_place, kv_sems)
     w_copies = []
     for d in range(1, n_head):
         to = head_peer(d)
@@ -162,7 +164,45 @@
                     to,
                 )
             )
-    for copy in x_copies + w_copies:
+    for copy in w_copies:
+        copy.start()
+    locals_ = [
+        pltpu.make_async_copy(
+            x_ref.at[:, pl.ds(pl.multiple_of(me * cols, cols), cols)],
+            x_all.at[own],
+            local_sem.at[0],
+        )
+    ]
+    own_feats = pl.ds(pl.multiple_of(head * feats, feats), feats)
+    for i, ref in enumerate((kw_ref, vw_ref)):
+        locals_.append(
+            pltpu.make_async_copy(
+                ref.at[own_feats],
+                w_all.at[:, pl.ds(pl.multiple_of((head * 2 + i) * HD, HD), HD)],
+                local_sem.at[1 + i],
+            )
+        )
+    for copy in locals_:
+        copy.start()
+    kv_all[pl.ds(2 * me, 2)] = kv_ref[...]
+    gather_on(kv_direct, kv_passed, kv_place, kv_sems)
+
+    quarter = half // 4
+    direct_first = core * half + side * quarter
+    x_copies = []
+    for d in range(1, n_ctx):
+        first = ctx_peer(d) * cols + direct_first
+        x_copies.append(
+            ctx_copy(
+                x_ref.at[:, pl.ds(pl.multiple_of(first, quarter), half - quarter)],
+                x_all.at[own, pl.ds(pl.multiple_of(direct_first, quarter), half - quarter)],
+                x_send,
+                x_recv,
+                d,
+                ctx_peer(d),
+            )
+        )
+    for copy in x_copies:
         copy.start()
 
     def sort_block(u, carry):
@@ -276,17 +316,33 @@
 
     lax.fori_loop(0, blocks, unsort, 0)
 
+    pair_sums = []
+    for k in range(strides):
+        target = lax.rem(ctx_partner + 2 * k, n_ctx)
+        to_rows = pl.ds(pl.multiple_of(target * tokens, tokens), tokens)
+        pair_sums.append(
+            ctx_copy(
+                part.at[to_rows], paired.at[k], sum_pair_send, sum_pair_recv, k, ctx_partner
+            )
+        )
+    order = list(range(1, strides)) + [0]
+    for k in order:
+        pair_sums[k].start()
     sums = []
-    for d in range(1, n_ctx):
-        to_rows = pl.ds(pl.multiple_of(ctx_peer(d) * tokens, tokens), tokens)
-        sums.append(ctx_copy(part.at[to_rows], received.at[d], sum_send, sum_recv, d))
-    for copy in sums:
-        copy.start()
-    for copy in sums:
-        copy.wait()
-    total = part[own, :].astype(jnp.float32)
-    for d in range(1, n_ctx):
-        total = total + received[d].astype(jnp.float32)
+    for k in order:
+        pair_sums[k].wait()
+        rows = pl.ds(pl.multiple_of(ctx_peer(2 * k) * tokens, tokens), tokens)
+        total = part[rows, :].astype(jnp.float32) + paired[k].astype(jnp.float32)
+        if k:
+            outgoing[k] = total.astype(jnp.bfloat16)
+            copy = ctx_copy(
+                outgoing.at[k], received.at[k], sum_send, sum_recv, k, ctx_peer(2 * k)
+            )
+            copy.start()
+            sums.append(copy)
+    for k in range(1, strides):
+        sums[k - 1].wait()
+        total = total + received[k].astype(jnp.float32)
     own_rows[...] = total.astype(jnp.bfloat16)
 
     head_cols = pl.ds(pl.multiple_of(head * 2 * HD, 2 * HD), 2 * HD)
@@ -294,9 +350,12 @@
     locals_.append(pltpu.make_async_copy(own_rows, rows_heads.at[:, head_cols], local_sem.at[4]))
     for copy in locals_[3:]:
         copy.start()
-    rows_copies = [
-        ctx_copy(own_rows, rows_all.at[own], rows_send, rows_recv, d) for d in range(1, n_ctx)
-    ]
+    def rows_place(source):
+        return rows_all.at[pl.ds(pl.multiple_of(source * tokens, tokens), tokens)]
+
+    rows_sems = (rows_send, rows_recv, rows_pair_send, rows_pair_recv)
+    rows_direct, rows_passed = gather(own_rows, rows_place, rows_sems)
+    rows_copies = []
     for d in range(1, n_head):
         rows_copies.append(
             head_copy(
@@ -306,15 +365,29 @@
     for copy in rows_copies:
         copy.start()
 
+    def x_piece(d, first, size):
+        return x_all.at[
+            pl.ds(pl.multiple_of(ctx_source(d) * tokens, tokens), tokens),
+            pl.ds(pl.multiple_of(first, quarter), size),
+        ]
+
+    side_copies = []
     pair_copies = []
     for d in range(1, n_ctx):
         x_copies[d - 1].wait()
-        source = ctx_source(d)
-        piece = x_all.at[
-            pl.ds(pl.multiple_of(source * tokens, tokens), tokens),
-            pl.ds(pl.multiple_of(core * half, half), half),
-        ]
+        edge = x_piece(d, core * half + side * 3 * quarter, quarter)
+        copy = head_copy(edge, edge, side_send, side_recv, d, across)
+        copy.start()
+        side_copies.append(copy)
+        piece = x_piece(d, direct_first, half - quarter)
         copy = head_copy(piece, piece, pair_send, pair_recv, d, partner)
+        copy.start()
+        pair_copies.append(copy)
+    gather_on(rows_direct, rows_passed, rows_place, rows_sems)
+    for d in range(1, n_ctx):
+        side_copies[d - 1].wait()
+        piece = x_piece(d, core * half + (1 - side) * 3 * quarter, quarter)
+        copy = head_copy(piece, piece, side_pair_send, side_pair_recv, d, partner)
         copy.start()
         pair_copies.append(copy)
     for copy in w_copies + rows_copies + pair_copies + locals_:
@@ -371,6 +444,14 @@
             pltpu.VMEM((seq, 2 * HD), bf16),
             pltpu.VMEM((n_ctx, tokens, 2 * HD), bf16),
             pltpu.VMEM((tokens, 2 * HD), bf16),
+            pltpu.VMEM((n_ctx // 2, tokens, 2 * HD), bf16),
+            pltpu.VMEM((n_ctx // 2, tokens, 2 * HD), bf16),
+            dma((n_ctx,)),
+            dma((n_ctx,)),
+            dma((n_ctx,)),
+            dma((n_ctx,)),
+            dma((n_ctx,)),
+            dma((n_ctx,)),
             dma((n_ctx,)),
             dma((n_ctx,)),
             dma((n_ctx,)),
@@ -379,6 +460,10 @@
             dma((n_ctx,)),
             dma((2 * n_head,)),
             dma((2 * n_head,)),
+            dma((n_ctx,)),
+            dma((n_ctx,)),
+            dma((n_ctx,)),
+            dma((n_ctx,)),
             dma((n_ctx,)),
             dma((n_ctx,)),
             dma((n_ctx,)),

time: 210 us -> 151 us (0.72)
  the two profiles are of different devices: /device:TPU:14 before, /device:TPU:29 now
where the time goes in v2:
time: 151 us
  Pallas kernels  134 us (89%)
  matrix products  9.83 us (7%)
  local copies, waits for them, and re-layouts  5.7 us (4%)
    pallas_call x1, Pallas kernels, local(): pl.pallas_call(functools.partial(kernel, n_ctx, n_head), out_shape=(jax.S...  134 us
    dot_general x1, matrix products, local(): lax.dot_general(x_all, rows_all, contract, preferred_element_type=f32)  6.14 us
    unnamed x8, local copies, waits for them, and re-layouts  4.17 us
    dot_general x1, matrix products, local(): lax.dot_general(rows_heads, w_all, NT, preferred_element_type=f32)  3.69 us

profile of v2, /device:TPU:29, one launch (start us, length us, event | category | flops | bytes accessed | tf_op | source)
XLA Modules:
  0.0 150.8 jit_solution(14933761875791647260)
XLA Ops:
  0.6 0.8 copy.14
  1.4 0.1 reshape.15.table
  1.5 0.1 select_reduce_fusion.inverse
  1.6 0.9 pad_maximum_fusion
  2.5 0.0 copy-start
  2.5 1.2 copy-done
  3.7 0.0 copy-start.1
  3.7 1.2 copy-done.1
  4.9 133.6 %shard_map.111 = (bf16[256,2048]{1,0:T(8,128)(2,1)S(1)}, bf16[2048,2048]{1,0:T(8,128)(2,1)}, bf16[4096,1024]{1,0:T(8,128)(2,1)}, bf16[2048,256]{1,0:T(8,128)(2,1)S(1)}, bf16[256,1024]{1,0:T(8,128)(2,1)S(1)}) custom-call(s32[16]{0:T(128)S(1)} %reshape.15.table, s32[16]{0:T(128)S(1)} %select_reduce_fusion.inverse, bf16[256,2048]{1,0:T(8,128)(2,1)S(1)} %copy-done, ...), custom_call_target="tpu_custom_call" | custom-call | tf_op jit(solution)/shard_map/pallas_call | solution.py:424
  138.5 0.0 copy-start.2
  138.6 6.1 %fusion.1 = f32[2048,256]{1,0:T(8,128)S(1)} fusion(bf16[2048,2048]{1,0:T(8,128)(2,1)} %get-tuple-element.10, bf16[2048,256]{1,0:T(8,128)(2,1)S(1)} %get-tuple-element.11), kind=kOutput, calls=%fused_computation.5 | convolution fusion | flops 2147483648 | bytes 11534336 | tf_op jit(solution)/shard_map/dot_general | solution.py:480
  144.7 1.5 fusion
  146.1 0.0 copy-done.2
  146.2 3.7 %convolution_convert_fusion = bf16[256,4096]{1,0:T(8,128)(2,1)} fusion(bf16[256,1024]{1,0:T(8,128)(2,1)S(1)} %get-tuple-element.12, bf16[4096,1024]{1,0:T(8,128)(2,1)S(1)} %copy-done.2), kind=kOutput, calls=%fused_computation | convolution fusion | flops 2148532224 | bytes 11010048 | tf_op jit(solution)/shard_map/dot_general | solution.py:481
  149.8 1.0 copy.16
Async XLA Ops:
  2.5 1.2 copy-start
  3.7 1.2 copy-start.1
  138.5 7.6 %copy-start.2 = (bf16[4096,1024]{1,0:T(8,128)(2,1)S(1)}, bf16[4096,1024]{1,0:T(8,128)(2,1)}, u32[]{:S(2)}) copy-start(bf16[4096,1024]{1,0:T(8,128)(2,1)} %get-tuple-element.13) | copy-start | bytes 25165828

commit v3 on v2

--- a/solution.py
+++ b/solution.py
@@ -328,6 +328,27 @@
     order = list(range(1, strides)) + [0]
     for k in order:
         pair_sums[k].start()
+    def x_piece(d, first, size):
+        return x_all.at[
+            pl.ds(pl.multiple_of(ctx_source(d) * tokens, tokens), tokens),
+            pl.ds(pl.multiple_of(first, quarter), size),
+        ]
+
+    side_copies = []
+    pair_copies = []
+    def forward(d):
+        x_copies[d - 1].wait()
+        edge = x_piece(d, core * half + side * 3 * quarter, quarter)
+        copy = head_copy(edge, edge, side_send, side_recv, d, across)
+        copy.start()
+        side_copies.append(copy)
+        piece = x_piece(d, direct_first, half - quarter)
+        copy = head_copy(piece, piece, pair_send, pair_recv, d, partner)
+        copy.start()
+        pair_copies.append(copy)
+
+    for d in range(1, strides):
+        forward(d)
     sums = []
     for k in order:
         pair_sums[k].wait()
@@ -365,24 +386,8 @@
     for copy in rows_copies:
         copy.start()
 
-    def x_piece(d, first, size):
-        return x_all.at[
-            pl.ds(pl.multiple_of(ctx_source(d) * tokens, tokens), tokens),
-            pl.ds(pl.multiple_of(first, quarter), size),
-        ]
-
-    side_copies = []
-    pair_copies = []
-    for d in range(1, n_ctx):
-        x_copies[d - 1].wait()
-        edge = x_piece(d, core * half + side * 3 * quarter, quarter)
-        copy = head_copy(edge, edge, side_send, side_recv, d, across)
-        copy.start()
-        side_copies.append(copy)
-        piece = x_piece(d, direct_first, half - quarter)
-        copy = head_copy(piece, piece, pair_send, pair_recv, d, partner)
-        copy.start()
-        pair_copies.append(copy)
+    for d in range(strides, n_ctx):
+        forward(d)
     gather_on(rows_direct, rows_passed, rows_place, rows_sems)
     for d in range(1, n_ctx):
         side_copies[d - 1].wait()

time: 151 us -> 145 us (0.960); the launches traced: 151 us -> 142 us
  Pallas kernels: 134 us -> 125 us
    pallas_call x1, Pallas kernels: 134 us -> 125 us  [local(): pl.pallas_call(functools.partial(kernel, n_ctx, n_head), out_shape=(jax.S...]
where the time goes in v3:
time: 145 us; the launch traced here: 142 us
  Pallas kernels  125 us (86%)
  matrix products  9.83 us (7%)
  local copies, waits for them, and re-layouts  5.7 us (4%)
    pallas_call x1, Pallas kernels, local(): pl.pallas_call(functools.partial(kernel, n_ctx, n_head), out_shape=(jax.S...  125 us
    dot_general x1, matrix products, local(): lax.dot_general(x_all, rows_all, contract, preferred_element_type=f32)  6.14 us
    unnamed x8, local copies, waits for them, and re-layouts  4.17 us
    dot_general x1, matrix products, local(): lax.dot_general(rows_heads, w_all, NT, preferred_element_type=f32)  3.69 us

profile of v3, /device:TPU:29, one launch (start us, length us, event | category | flops | bytes accessed | tf_op | source)
XLA Modules:
  0.0 142.4 jit_solution(16445766825180202047)
XLA Ops:
  0.6 0.8 copy.14
  1.4 0.1 reshape.15.table
  1.5 0.1 select_reduce_fusion.inverse
  1.6 0.9 pad_maximum_fusion
  2.5 0.0 copy-start
  2.5 1.2 copy-done
  3.7 0.0 copy-start.1
  3.7 1.2 copy-done.1
  4.9 125.2 %shard_map.111 = (bf16[256,2048]{1,0:T(8,128)(2,1)S(1)}, bf16[2048,2048]{1,0:T(8,128)(2,1)}, bf16[4096,1024]{1,0:T(8,128)(2,1)}, bf16[2048,256]{1,0:T(8,128)(2,1)S(1)}, bf16[256,1024]{1,0:T(8,128)(2,1)S(1)}) custom-call(s32[16]{0:T(128)S(1)} %reshape.15.table, s32[16]{0:T(128)S(1)} %select_reduce_fusion.inverse, bf16[256,2048]{1,0:T(8,128)(2,1)S(1)} %copy-done, ...), custom_call_target="tpu_custom_call" | custom-call | tf_op jit(solution)/shard_map/pallas_call | solution.py:429
  130.1 0.0 copy-start.2
  130.1 6.1 %fusion.1 = f32[2048,256]{1,0:T(8,128)S(1)} fusion(bf16[2048,2048]{1,0:T(8,128)(2,1)} %get-tuple-element.10, bf16[2048,256]{1,0:T(8,128)(2,1)S(1)} %get-tuple-element.11), kind=kOutput, calls=%fused_computation.5 | convolution fusion | flops 2147483648 | bytes 11534336 | tf_op jit(solution)/shard_map/dot_general | solution.py:485
  136.3 1.5 %fusion = (f32[2048,128]{1,0:T(8,128)}, f32[2048,128]{1,0:T(8,128)}) fusion(f32[2048,256]{1,0:T(8,128)S(1)} %fusion.1), kind=kLoop, calls=%fused_computation.4 | loop fusion | bytes 4194304 | tf_op jit(solution)/shard_map/slice | solution.py:487
  137.7 0.0 copy-done.2
  137.7 3.7 %convolution_convert_fusion = bf16[256,4096]{1,0:T(8,128)(2,1)} fusion(bf16[256,1024]{1,0:T(8,128)(2,1)S(1)} %get-tuple-element.12, bf16[4096,1024]{1,0:T(8,128)(2,1)S(1)} %copy-done.2), kind=kOutput, calls=%fused_computation | convolution fusion | flops 2148532224 | bytes 11010048 | tf_op jit(solution)/shard_map/dot_general | solution.py:486
  141.4 1.0 copy.16
Async XLA Ops:
  2.5 1.2 copy-start
  3.7 1.2 copy-start.1
  130.1 7.6 %copy-start.2 = (bf16[4096,1024]{1,0:T(8,128)(2,1)S(1)}, bf16[4096,1024]{1,0:T(8,128)(2,1)}, u32[]{:S(2)}) copy-start(bf16[4096,1024]{1,0:T(8,128)(2,1)} %get-tuple-element.13) | copy-start | bytes 25165828
